TPU v7x, 128 devices: a whole 4x4x4 slice. The times are simulated.
128 devices in a mesh: tm: 8 (over z, core), rows: 16 (over y, x).
Axes of the slice: x: 4, y: 4, z: 4, core: 2. Of those that a mesh axis runs over, the one named last changes fastest.
Arguments:
- latent: bfloat16 [16, 32, 48, 512], P('tm', 'rows'), may hold values from -24 to 24, as said below
- gain_first: float32 [512], replicated, may hold values from 0.1 to 1.9
- shift_first: float32 [512], replicated, may hold values from -0.5 to 0.5
- kernel_first: bfloat16 [3, 3, 3, 512, 256], replicated, may hold values from -0.0546875 to 0.0546875
- gain_second: float32 [256], replicated, may hold values from 0.1 to 1.9
- shift_second: float32 [256], replicated, may hold values from -0.5 to 0.5
- kernel_second: bfloat16 [3, 3, 3, 256, 256], replicated, may hold values from -0.078125 to 0.078125
Outputs:
- decoded: bfloat16 [32, 64, 96, 256], P('tm', 'rows')
Inputs may be any that keep to these rules, and one draw needn't show every extreme that they name: `latent`: real-valued features.
All inputs are finite; a program needn't handle non-finite values.
Results may differ from a plain program's by a relative error of at most 0.015.
Values may be sent and summed in bfloat16 or wider, within the bound.
A program may use at most 64 MiB of HBM per device.

v0:
```python
import jax
import jax.numpy as jnp
from jax import lax
from jax.sharding import PartitionSpec as P

GROUPS = 32


EPS = 1e-06


def shifted(block, axis, distance):
    devices = range(lax.axis_size(axis))
    route = [(i - distance, i) for i in devices if i - distance in devices]
    return lax.ppermute(block, axis, route)


def padded_2(array, sides, width):
    for axis, dim in sides:
        peers, length = (lax.axis_size(axis), array.shape[dim])
        up = [(i, (i + 1) % peers) for i in range(peers - 1)]
        down = [(j, i) for i, j in up]
        last = lax.slice_in_dim(array, length - width, length, axis=dim)
        initial = lax.slice_in_dim(array, 0, width, axis=dim)
        before = lax.ppermute(last, axis, up)
        after = lax.ppermute(initial, axis, down)
        array = jnp.concatenate([before, array, after], axis=dim)
    return array


def channel_stats(values, groups):
    chans = values.shape[-1]
    flat = values.reshape(-1, chans)
    total = jnp.sum(flat, axis=0).reshape(groups, -1).sum(axis=1)
    square = jnp.sum(flat * flat, axis=0).reshape(groups, -1).sum(axis=1)
    return lax.psum((total, square), ("tm", "rows"))


def normalize(values, total, square, count, gain, shift, groups):
    chans = values.shape[-1]
    mean = total / count
    spread = square / count - mean * mean
    scale = lax.rsqrt(spread + EPS)
    mean_c = jnp.repeat(mean, chans // groups)
    scale_c = jnp.repeat(scale, chans // groups)
    inner = (values.astype(jnp.float32) - mean_c) * scale_c * gain + shift
    return jax.nn.silu(inner).astype(jnp.bfloat16)


def convolve(padded, kernel, frames, height, width):
    cin = padded.shape[-1]
    cout = kernel.shape[-1]
    total = jnp.zeros((frames * height * width, cout), jnp.float32)
    for ta in range(3):
        for hb in range(3):
            for wc in range(3):
                piece = padded[ta : ta + frames, hb : hb + height, wc : wc + width].reshape(-1, cin)
                total = total + jnp.dot(
                    piece, kernel[ta, hb, wc], preferred_element_type=jnp.float32
                )
    return total.reshape(frames, height, width, cout)


def upsample(values):
    values = jnp.repeat(values, 2, axis=0)
    values = jnp.repeat(values, 2, axis=1)
    return jnp.repeat(values, 2, axis=2)


def per_device(
    latent, gain_first, shift_first, kernel_first, gain_second, shift_second, kernel_second
):
    frames, height, width, cin = latent.shape
    cout = kernel_first.shape[-1]
    groups = GROUPS
    devices = lax.axis_size("tm") * lax.axis_size("rows")
    total, square = channel_stats(latent.astype(jnp.float32), groups)
    count = devices * frames * height * width * (cin // groups)
    first = normalize(latent, total, square, count, gain_first, shift_first, groups)
    cache = shifted(first, "tm", 1)
    extended = jnp.concatenate([cache, first], axis=0)
    banded = padded_2(extended, (("rows", 1),), 1)
    padded = jnp.pad(banded, ((0, 0), (0, 0), (1, 1), (0, 0)))
    middle = convolve(padded, kernel_first, frames, height, width).astype(jnp.bfloat16)
    total, square = channel_stats(middle.astype(jnp.float32), groups)
    count = devices * frames * height * width * (cout // groups)
    second = normalize(middle, total, square, count, gain_second, shift_second, groups)
    upsampled = upsample(second)
    cache = shifted(upsampled[2 * frames - 2 :], "tm", 1)
    extended = jnp.concatenate([cache, upsampled], axis=0)
    banded = padded_2(extended, (("rows", 1),), 1)
    padded = jnp.pad(banded, ((0, 0), (0, 0), (1, 1), (0, 0)))
    decoded = convolve(padded, kernel_second, 2 * frames, 2 * height, 2 * width)
    return decoded.astype(jnp.bfloat16)


def solution(mesh):
    placed = (P("tm", "rows", None, None), P(), P(), P(), P(), P(), P())
    return jax.shard_map(
        per_device,
        mesh=mesh,
        in_specs=placed,
        out_specs=P("tm", "rows", None, None),
        check_vma=False,
    )
```

profile of v0, /device:TPU:38, one launch (start us, length us, event | category | flops | bytes accessed | tf_op | source)
XLA Modules:
  0.0 203.6 jit_solution(16145684296686891112)
XLA Ops:
  0.0 1.0 convert_reduce_fusion
  1.4 65.4 %all-reduce.3 = (f32[32]{0:T(128)S(1)}, f32[32]{0:T(128)S(1)}) all-reduce(f32[32]{0:T(128)S(1)} %reduce_sum.75, f32[32]{0:T(128)S(1)} %reduce_sum.73), channel_id=1, replica_groups=mesh['tm'=8,'rows'=16] {'tm','rows'}, use_global_device_ids=true, to_apply=%region_5.0 | all-reduce | flops 64 | bytes 512 | tf_op jit(solution)/shard_map/psum | solution.py:36
  67.1 1.1 fusion.29
  68.2 1.9 collective-permute-start
  70.2 5.1 %collective-permute-done = bf16[2,2,48,512]{3,2,1,0:T(8,128)(2,1)S(1)} collective-permute-done((bf16[2,2,48,512]{3,2,1,0:T(8,128)(2,1)S(1)}, bf16[2,2,48,512]{3,2,1,0:T(8,128)(2,1)S(1)}, u32[]{:S(2)}, u32[]{:S(2)}) %collective-permute-start) | collective-permute-done | bytes 196640 | tf_op jit(solution)/shard_map/ppermute | solution.py:15
  75.3 3.1 %collective-permute-start.1 = (bf16[4,1,48,512]{3,2,1,0:T(8,128)(2,1)S(1)}, bf16[4,1,48,512]{3,2,1,0:T(8,128)(2,1)S(1)}, u32[]{:S(2)}, u32[]{:S(2)}) collective-permute-start(bf16[4,1,48,512]{3,2,1,0:T(8,128)(2,1)S(1)} %get-tuple-element.70), channel_id=1, source_target_pairs={{0,1},{1,2},{2,3},{3,4},{4,5},{5,6},{6,7},{7,8},{8,9},{9,10},{10,1... | collective-permute-start | bytes 589832 | tf_op jit(solution)/shard_map/ppermute | solution.py:25
  78.4 2.8 %collective-permute-start.2 = (bf16[4,1,48,512]{3,2,1,0:T(8,128)(2,1)S(1)}, bf16[4,1,48,512]{3,2,1,0:T(8,128)(2,1)S(1)}, u32[]{:S(2)}, u32[]{:S(2)}) collective-permute-start(bf16[4,1,48,512]{3,2,1,0:T(8,128)(2,1)S(1)} %get-tuple-element.71), channel_id=1, source_target_pairs={{1,0},{2,1},{3,2},{4,3},{5,4},{6,5},{7,6},{8,7},{9,8},{10,9},{11,1... | collective-permute-start | bytes 589832 | tf_op jit(solution)/shard_map/ppermute | solution.py:26
  81.2 1.7 collective-permute-done.1
  82.8 5.2 %collective-permute-done.2 = bf16[4,1,48,512]{3,2,1,0:T(8,128)(2,1)S(1)} collective-permute-done((bf16[4,1,48,512]{3,2,1,0:T(8,128)(2,1)S(1)}, bf16[4,1,48,512]{3,2,1,0:T(8,128)(2,1)S(1)}, u32[]{:S(2)}, u32[]{:S(2)}) %collective-permute-start.2) | collective-permute-done | bytes 196640 | tf_op jit(solution)/shard_map/ppermute | solution.py:26
  88.4 0.6 fusion.150
  89.0 2.4 %copy-done = bf16[3,3,3,512,256]{4,3,2,1,0:T(8,128)(2,1)S(1)} copy-done((bf16[3,3,3,512,256]{4,3,2,1,0:T(8,128)(2,1)S(1)}, bf16[3,3,3,512,256]{4,3,2,1,0:T(8,128)(2,1)}, u32[]{:S(2)}) %copy-start) | copy-done | bytes 7077912
  98.0 62.7 %all-reduce.2 = (f32[32]{0:T(128)S(1)}, f32[32]{0:T(128)S(1)}) all-reduce(f32[32]{0:T(128)S(1)} %reduce_sum.79, f32[32]{0:T(128)S(1)} %reduce_sum.77), channel_id=1, replica_groups=mesh['tm'=8,'rows'=16] {'tm','rows'}, use_global_device_ids=true, to_apply=%region_11.12 | all-reduce | flops 64 | bytes 512 | tf_op jit(solution)/shard_map/psum | solution.py:36
  161.4 1.9 collective-permute-start.3
  163.4 0.7 broadcast_in_dim.46
  164.4 6.1 %collective-permute-done.3 = bf16[2,4,96,256]{3,2,1,0:T(8,128)(2,1)S(1)} collective-permute-done((bf16[2,4,96,256]{3,2,1,0:T(8,128)(2,1)S(1)}, bf16[2,4,96,256]{3,2,1,0:T(8,128)(2,1)S(1)}, u32[]{:S(2)}, u32[]{:S(2)}) %collective-permute-start.3) | collective-permute-done | bytes 393248 | tf_op jit(solution)/shard_map/ppermute | solution.py:15
  170.6 0.8 fusion.149
  171.4 3.2 %collective-permute-start.4 = (bf16[6,1,96,256]{3,2,1,0:T(8,128)(2,1)}, bf16[6,1,96,256]{3,2,1,0:T(8,128)(2,1)S(1)}, u32[]{:S(2)}, u32[]{:S(2)}) collective-permute-start(bf16[6,1,96,256]{3,2,1,0:T(8,128)(2,1)} %get-tuple-element.42), channel_id=1, source_target_pairs={{0,1},{1,2},{2,3},{3,4},{4,5},{5,6},{6,7},{7,8},{8,9},{9,10},{10,1... | collective-permute-start | bytes 884744 | tf_op jit(solution)/shard_map/ppermute | solution.py:25
  174.7 2.8 %collective-permute-start.5 = (bf16[6,1,96,256]{3,2,1,0:T(8,128)(2,1)}, bf16[6,1,96,256]{3,2,1,0:T(8,128)(2,1)S(1)}, u32[]{:S(2)}, u32[]{:S(2)}) collective-permute-start(bf16[6,1,96,256]{3,2,1,0:T(8,128)(2,1)} %get-tuple-element.43), channel_id=1, source_target_pairs={{1,0},{2,1},{3,2},{4,3},{5,4},{6,5},{7,6},{8,7},{9,8},{10,9},{11,1... | collective-permute-start | bytes 884744 | tf_op jit(solution)/shard_map/ppermute | solution.py:26
  177.8 2.7 %collective-permute-done.4 = bf16[6,1,96,256]{3,2,1,0:T(8,128)(2,1)S(1)} collective-permute-done((bf16[6,1,96,256]{3,2,1,0:T(8,128)(2,1)}, bf16[6,1,96,256]{3,2,1,0:T(8,128)(2,1)S(1)}, u32[]{:S(2)}, u32[]{:S(2)}) %collective-permute-start.4) | collective-permute-done | bytes 294944 | tf_op jit(solution)/shard_map/ppermute | solution.py:25
  180.5 5.9 %collective-permute-done.5 = bf16[6,1,96,256]{3,2,1,0:T(8,128)(2,1)S(1)} collective-permute-done((bf16[6,1,96,256]{3,2,1,0:T(8,128)(2,1)}, bf16[6,1,96,256]{3,2,1,0:T(8,128)(2,1)S(1)}, u32[]{:S(2)}, u32[]{:S(2)}) %collective-permute-start.5) | collective-permute-done | bytes 294944 | tf_op jit(solution)/shard_map/ppermute | solution.py:26
  186.4 1.0 fusion.8
  187.4 4.5 %fusion.148 = (bf16[4,4,96,256]{3,2,1,0:T(8,128)(2,1)S(1)}, bf16[4,4,96,256]{3,2,1,0:T(8,128)(2,1)S(1)}, bf16[4,4,96,256]{3,2,1,0:T(8,128)(2,1)S(1)}, bf16[4,4,9...) fusion(bf16[6,6,98,256]{3,2,1,0:T(8,128)(2,1)S(1)} %fusion.8), kind=kLoop, calls=%fused_computation.231 | loop fusion | bytes 28311552 | tf_op jit(solution)/shard_map/slice | solution.py:57
  192.3 0.4 fusion.97
  192.7 0.4 fusion.90
  193.1 0.6 pad_maximum_fusion
  193.6 0.4 convolution_add_fusion.23
  194.0 0.4 convolution_add_fusion.22
  194.4 0.4 convolution_add_fusion.21
  194.7 0.4 convolution_add_fusion.20
  195.1 0.4 convolution_add_fusion.19
  195.5 0.4 convolution_add_fusion.18
  195.9 0.4 convolution_add_fusion.17
  196.2 0.4 convolution_add_fusion.16
  196.6 0.4 convolution_add_fusion.15
  197.0 0.4 convolution_add_fusion.14
  197.3 0.4 convolution_add_fusion.13
  197.7 0.4 convolution_add_fusion.12
  198.1 0.4 convolution_add_fusion.11
  198.4 0.4 convolution_add_fusion.10
  198.8 0.4 convolution_add_fusion.9
  199.2 0.4 convolution_add_fusion.8
  199.6 0.4 convolution_add_fusion.7
  199.9 0.4 convolution_add_fusion.6
  200.3 0.5 fusion.2
  200.8 0.4 convolution_add_fusion.4
  201.1 0.4 convolution_add_fusion.3
  201.9 0.4 convolution_add_fusion.1
  202.3 1.3 fusion.3
  (71 shorter events, 9.5 us)
Async XLA Ops:
  68.2 7.0 %collective-permute-start = (bf16[2,2,48,512]{3,2,1,0:T(8,128)(2,1)S(1)}, bf16[2,2,48,512]{3,2,1,0:T(8,128)(2,1)S(1)}, u32[]{:S(2)}, u32[]{:S(2)}) collective-permute-start(bf16[2,2,48,512]{3,2,1,0:T(8,128)(2,1)S(1)} %fusion.29), channel_id=1, source_target_pairs={{0,16},{16,32},{32,48},{48,64},{64,80},{80,96},{96,112},{1,17},{17... | collective-permute-start | bytes 589832 | tf_op jit(solution)/shard_map/ppermute | solution.py:15
  75.3 7.6 %collective-permute-start.1 = (bf16[4,1,48,512]{3,2,1,0:T(8,128)(2,1)S(1)}, bf16[4,1,48,512]{3,2,1,0:T(8,128)(2,1)S(1)}, u32[]{:S(2)}, u32[]{:S(2)}) collective-permute-start(bf16[4,1,48,512]{3,2,1,0:T(8,128)(2,1)S(1)} %get-tuple-element.70), channel_id=1, source_target_pairs={{0,1},{1,2},{2,3},{3,4},{4,5},{5,6},{6,7},{7,8},{8,9},{9,10},{10,1... | collective-permute-start | bytes 589832 | tf_op jit(solution)/shard_map/ppermute | solution.py:25
  78.4 9.7 %collective-permute-start.2 = (bf16[4,1,48,512]{3,2,1,0:T(8,128)(2,1)S(1)}, bf16[4,1,48,512]{3,2,1,0:T(8,128)(2,1)S(1)}, u32[]{:S(2)}, u32[]{:S(2)}) collective-permute-start(bf16[4,1,48,512]{3,2,1,0:T(8,128)(2,1)S(1)} %get-tuple-element.71), channel_id=1, source_target_pairs={{1,0},{2,1},{3,2},{4,3},{5,4},{6,5},{7,6},{8,7},{9,8},{10,9},{11,1... | collective-permute-start | bytes 589832 | tf_op jit(solution)/shard_map/ppermute | solution.py:26
  88.4 3.0 %copy-start = (bf16[3,3,3,512,256]{4,3,2,1,0:T(8,128)(2,1)S(1)}, bf16[3,3,3,512,256]{4,3,2,1,0:T(8,128)(2,1)}, u32[]{:S(2)}) copy-start(bf16[3,3,3,512,256]{4,3,2,1,0:T(8,128)(2,1)} %param.10) | copy-start | bytes 21233668
  96.6 64.4 %copy-start.2 = (f32[256]{0:T(256)S(1)}, f32[256]{0:T(256)}, u32[]{:S(2)}) copy-start(f32[256]{0:T(256)} %param.12) | copy-start | bytes 3076
  96.6 64.4 %copy-start.3 = (f32[256]{0:T(256)S(1)}, f32[256]{0:T(256)}, u32[]{:S(2)}) copy-start(f32[256]{0:T(256)} %param.11) | copy-start | bytes 3076
  161.4 9.1 %collective-permute-start.3 = (bf16[2,4,96,256]{3,2,1,0:T(8,128)(2,1)S(1)}, bf16[2,4,96,256]{3,2,1,0:T(8,128)(2,1)S(1)}, u32[]{:S(2)}, u32[]{:S(2)}) collective-permute-start(bf16[2,4,96,256]{3,2,1,0:T(8,128)(2,1)S(1)} %broadcast_in_dim.43), channel_id=1, source_target_pairs={{0,16},{16,32},{32,48},{48,64},{64,80},{80,96},{96,112},{1,17},{17... | collective-permute-start | bytes 1179656 | tf_op jit(solution)/shard_map/ppermute | solution.py:15
  171.4 9.0 %collective-permute-start.4 = (bf16[6,1,96,256]{3,2,1,0:T(8,128)(2,1)}, bf16[6,1,96,256]{3,2,1,0:T(8,128)(2,1)S(1)}, u32[]{:S(2)}, u32[]{:S(2)}) collective-permute-start(bf16[6,1,96,256]{3,2,1,0:T(8,128)(2,1)} %get-tuple-element.42), channel_id=1, source_target_pairs={{0,1},{1,2},{2,3},{3,4},{4,5},{5,6},{6,7},{7,8},{8,9},{9,10},{10,1... | collective-permute-start | bytes 884744 | tf_op jit(solution)/shard_map/ppermute | solution.py:25
  174.7 11.7 %collective-permute-start.5 = (bf16[6,1,96,256]{3,2,1,0:T(8,128)(2,1)}, bf16[6,1,96,256]{3,2,1,0:T(8,128)(2,1)S(1)}, u32[]{:S(2)}, u32[]{:S(2)}) collective-permute-start(bf16[6,1,96,256]{3,2,1,0:T(8,128)(2,1)} %get-tuple-element.43), channel_id=1, source_target_pairs={{1,0},{2,1},{3,2},{4,3},{5,4},{6,5},{7,6},{8,7},{9,8},{10,9},{11,1... | collective-permute-start | bytes 884744 | tf_op jit(solution)/shard_map/ppermute | solution.py:26
  187.4 4.6 %copy-start.1 = (bf16[3,3,3,256,256]{4,3,2,1,0:T(8,128)(2,1)S(1)}, bf16[3,3,3,256,256]{4,3,2,1,0:T(8,128)(2,1)}, u32[]{:S(2)}) copy-start(bf16[3,3,3,256,256]{4,3,2,1,0:T(8,128)(2,1)} %param.13) | copy-start | bytes 10616836
where the time goes:
time: 204 us
  blocking collectives  128 us (63%)
  waiting for transfers between devices  26.7 us (13%)
  matrix products  16.6 us (8%)
  starting transfers between devices  15.7 us (8%)
  local copies, waits for them, and re-layouts  11 us (5%)
  other arithmetic  4.73 us (2%)
    psum x2, blocking collectives, channel_stats(): return lax.psum((total, square), ('tm', 'rows'))  128 us
    dot_general x54, matrix products, convolve(): jnp.dot(piece, kernel[ta, hb, wc], preferred_element_type=jnp.float32)  16.6 us
    ppermute x2, waiting for transfers between devices, shifted(): return lax.ppermute(block, axis, route)  11.2 us
    ppermute x2, waiting for transfers between devices, padded_2(): after = lax.ppermute(initial, axis, down)  11.1 us
    ppermute x2, starting transfers between devices, padded_2(): before = lax.ppermute(last, axis, up)  6.3 us
    ppermute x2, starting transfers between devices, padded_2(): after = lax.ppermute(initial, axis, down)  5.56 us
    slice x3, local copies, waits for them, and re-layouts, convolve(): padded[ta:ta + frames, hb:hb + height, wc:wc + width].reshape(-1, cin)  5.25 us
    ppermute x2, waiting for transfers between devices, padded_2(): before = lax.ppermute(last, axis, up)  4.38 us
  transfers between devices with their start and end apart: 6, of which 6 were waited for; matrix products, arithmetic and copies ran while one was open for 1% of the time, Pallas kernels for 0%

commit v1 on v0

v1 whole, which is shorter than its diff:
```python
import functools

import jax
import jax.numpy as jnp
from jax import lax
from jax.experimental import pallas as pl
from jax.experimental.pallas import tpu as pltpu
from jax.sharding import PartitionSpec as P

GROUPS = 32
EPS = 1e-06
MESH = pl.DeviceIdType.MESH
LANES = 128
TAPS = 3
CORES = 2
SIDE = 4


def chip_partners(tm, row, tm_n, rows_n):
    at_z = [lax.rem(tm + CORES * d, tm_n) for d in range(tm_n // CORES)]
    at_y = [lax.rem(row - lax.rem(row, SIDE) + SIDE * d, rows_n) for d in range(rows_n // SIDE)]
    at_x = [lax.rem(row + d, SIDE) for d in range(SIDE)]
    hops = lambda d, n: min(d, n - d)
    steps = [
        (-hops(dz, len(at_z)) - hops(dy, len(at_y)) - hops(dx, SIDE), dz, dy, dx)
        for dz in range(len(at_z))
        for dy in range(len(at_y))
        for dx in range(SIDE)
        if dz or dy or dx
    ]
    return [(at_z[dz], at_y[dy] + at_x[dx]) for _, dz, dy, dx in sorted(steps)]


def lane_sums(x, size):
    lane = lax.broadcasted_iota(jnp.int32, x.shape, 1)
    d = 1
    while d < size:
        other = jnp.where((lane & d) == 0, pltpu.roll(x, LANES - d, 1), pltpu.roll(x, d, 1))
        x = x + other
        d *= 2
    return x


def diagonal(size):
    lane = lax.broadcasted_iota(jnp.int32, (8, LANES), 1)
    sub = lax.broadcasted_iota(jnp.int32, (8, LANES), 0)
    return (lane & (size - 1)) == sub


def pack_stats(total, square):
    blocks = total.shape[1] // LANES
    size = total.shape[1] // GROUPS
    sub = lax.broadcasted_iota(jnp.int32, (8, LANES), 0)
    rows = jnp.zeros((8, LANES), jnp.float32)
    for v in range(blocks):
        part = slice(v * LANES, (v + 1) * LANES)
        rows = jnp.where(sub == v, total[:, part], rows)
        rows = jnp.where(sub == blocks + v, square[:, part], rows)
    rows = lane_sums(rows, size)
    return jnp.sum(jnp.where(diagonal(size), rows, 0.0), axis=0, keepdims=True)


def affine(packed, count, gain, shift):
    chans = gain.shape[1]
    blocks, size = chans // LANES, chans // GROUPS
    rows = jnp.where(diagonal(size), jnp.broadcast_to(packed, (8, LANES)), 0.0)
    rows = lane_sums(rows, size) * (1.0 / count)
    mean = rows
    spread = pltpu.roll(rows, 8 - blocks, 0) - mean * mean
    scale = lax.rsqrt(spread + EPS) * 0.5
    a = jnp.concatenate([scale[v : v + 1] for v in range(blocks)], axis=1) * gain
    m = jnp.concatenate([mean[v : v + 1] for v in range(blocks)], axis=1)
    return a, shift * 0.5 - m * a


def activate(x, a, b):
    half = x.astype(jnp.float32) * a + b
    return (half + half * jnp.tanh(half)).astype(jnp.bfloat16)


def kernel(
    tm_n, rows_n,
    latent, gain1, shift1, kernel1, gain2, shift2, kernel2, out,
    lx, xn, w1, w2, w2m, mx, sn, stage, ob, g1, s1, g2, s2, red_core, red_chip,
    load_sem, w1_sem, w2_sem, out_sem, hs_sem, hr_sem, rs_sem, rr_sem,
):
    tm, row = lax.axis_index("tm"), lax.axis_index("rows")
    frames, height, width, cin = latent.shape
    cout = kernel1.shape[-1]
    up_ok, down_ok = row > 0, row < rows_n - 1
    prev_ok, next_ok = tm > 0, tm < tm_n - 1
    tm_at = lambda d: lax.rem(tm + d + tm_n, tm_n)
    row_at = lambda d: lax.rem(row + d + rows_n, rows_n)

    own = lx.at[2:4, 1:3]
    load = pltpu.make_async_copy(latent, own, load_sem.at[0])
    load.start()
    small = [
        pltpu.make_async_copy(src, dst, load_sem.at[1 + n])
        for n, (src, dst) in enumerate(((gain1, g1), (shift1, s1), (gain2, g2), (shift2, s2)))
    ]
    for c in small:
        c.start()
    slot = (0, 4, 2)
    w2_loads, w1_loads = [], []
    for i in range(TAPS):
        w2_loads.append(pltpu.make_async_copy(kernel2.at[i, 0], w2.at[0, :, slot[i]], w2_sem.at[3 * i]))
        w2_loads.append(pltpu.make_async_copy(kernel2.at[i, 1], w2m.at[i], w2_sem.at[3 * i + 1]))
        w2_loads.append(pltpu.make_async_copy(kernel2.at[i, 2], w2.at[1, :, slot[i] + 1], w2_sem.at[3 * i + 2]))
    for i in range(TAPS):
        for k in range(TAPS):
            w1_loads.append(pltpu.make_async_copy(kernel1.at[i, :, k], w1.at[k, i], w1_sem.at[TAPS * i + k]))
    for c in w2_loads + w1_loads:
        c.start()

    barrier = pltpu.get_barrier_semaphore()
    chips = chip_partners(tm, row, tm_n, rows_n)
    twin = (tm + 1 - 2 * lax.rem(tm, CORES), row)
    partners = chips + [(tm_at(d), row_at(e)) for e in (-1, 1, 0) for d in (-1, 1)]
    for p in partners:
        pl.semaphore_signal(barrier, inc=1, device_id=p, device_id_type=MESH)
    pl.semaphore_wait(barrier, len(partners))

    both = jnp.logical_and
    peers = [
        (next_ok, (tm_at(1), row)),
        (up_ok, (tm, row_at(-1))),
        (down_ok, (tm, row_at(1))),
        (both(next_ok, up_ok), (tm_at(1), row_at(-1))),
        (both(next_ok, down_ok), (tm_at(1), row_at(1))),
    ]
    arrives = [prev_ok, down_ok, up_ok, both(prev_ok, down_ok), both(prev_ok, up_ok)]

    def exchange(which, sources, targets):
        copies = []
        for n in range(5):
            ok, device = peers[n]
            copy = pltpu.make_async_remote_copy(
                src_ref=sources[n], dst_ref=targets[n],
                send_sem=hs_sem.at[which, n], recv_sem=hr_sem.at[which, n],
                device_id=device, device_id_type=MESH,
            )
            pl.when(ok)(copy.start)
            copies.append(copy)
        return copies

    def send(which, ref, n, device):
        pltpu.make_async_remote_copy(
            src_ref=ref.at[0], dst_ref=ref.at[n],
            send_sem=rs_sem.at[which], recv_sem=rr_sem.at[which],
            device_id=device, device_id_type=MESH,
        ).start()

    def arrived(which, ref):
        n = ref.shape[0]
        pltpu.make_async_copy(ref.at[1:n], ref.at[1:n], rr_sem.at[which]).wait()
        return jnp.sum(ref[...], axis=0)

    def reduce_chip(which, value):
        ref = red_core.at[which]
        ref[0] = value
        send(2 * which, ref, 1, twin)

    def reduce_all(which):
        ref = red_chip.at[which]
        ref[0] = arrived(2 * which, red_core.at[which])
        for n, device in enumerate(chips):
            send(2 * which + 1, ref, n + 1, device)

    def reduced(which):
        return arrived(2 * which + 1, red_chip.at[which])

    boxes = [(0, 2, 1, 3), (2, 4, 3, 4), (2, 4, 0, 1), (0, 2, 3, 4), (0, 2, 0, 1)]
    halo1 = exchange(
        0,
        [latent, latent.at[:, 0:1], latent.at[:, 1:2], latent.at[:, 0:1], latent.at[:, 1:2]],
        [lx.at[a:b, c:d] for a, b, c, d in boxes],
    )
    load.wait()
    x = lx[2:4, 1:3].astype(jnp.float32).reshape(frames * height * width, cin)
    reduce_chip(0, pack_stats(jnp.sum(x, axis=0, keepdims=True), jnp.sum(x * x, axis=0, keepdims=True)))
    reduce_all(0)
    for c in w2_loads:
        c.wait()

    def merge(i):
        for k in range(TAPS):
            mid = w2m[i, k].astype(jnp.float32)
            w2[0, k, slot[i] + 1] = (mid + w2[1, k, slot[i] + 1].astype(jnp.float32)).astype(jnp.bfloat16)
            w2[1, k, slot[i]] = (mid + w2[0, k, slot[i]].astype(jnp.float32)).astype(jnp.bfloat16)

    for i in range(TAPS):
        merge(i)
    for c in small:
        c.wait()
    count = tm_n * rows_n * frames * height * width * (cin // GROUPS)
    a, b = affine(reduced(0), count, g1[...], s1[...])

    def normalize(source, target, box, a, b):
        f0, f1, r0, r1 = box
        for f in range(f0, f1):
            for r in range(r0, r1):
                target[f, r] = activate(source[f, r], a, b)

    def normalize_halo(n, copy, source, target, box, a, b):
        f0, f1, r0, r1 = box

        @pl.when(arrives[n])
        def _():
            copy.wait_recv()
            normalize(source, target, box, a, b)

        @pl.when(jnp.logical_not(arrives[n]))
        def _():
            target[f0:f1, r0:r1] = jnp.zeros((f1 - f0, r1 - r0) + target.shape[2:], target.dtype)

    normalize(lx, xn, (2, 4, 1, 3), a, b)
    for n in range(5):
        normalize_halo(n, halo1[n], lx, xn, boxes[n], a, b)
    for c in w1_loads:
        c.wait()

    size = frames * height * width
    column = lax.rem(lax.broadcasted_iota(jnp.int32, (size, cout), 0), width)
    after = lambda y: jnp.where(column == 0, 0.0, pltpu.roll(y, 1, 0))
    before = lambda y: jnp.where(column == width - 1, 0.0, pltpu.roll(y, size - 1, 0))

    lhs = jnp.concatenate(
        [xn[i : i + frames, j : j + height].reshape(size, cin) for i in range(TAPS) for j in range(TAPS)], axis=1
    )
    y = [
        jnp.dot(lhs, w1[k].reshape(TAPS * TAPS * cin, cout), preferred_element_type=jnp.float32)
        for k in range(TAPS)
    ]
    middle = (after(y[0]) + y[1] + before(y[2])).astype(jnp.bfloat16)
    mx[1:3, 1:3] = middle.reshape(frames, height, width, cout)

    boxes = [(0, 1, 1, 3), (1, 3, 3, 4), (1, 3, 0, 1), (0, 1, 3, 4), (0, 1, 0, 1)]
    halo2 = exchange(
        1,
        [mx.at[2:3, 1:3], mx.at[1:3, 1:2], mx.at[1:3, 2:3], mx.at[2:3, 1:2], mx.at[2:3, 2:3]],
        [mx.at[a:b, c:d] for a, b, c, d in boxes],
    )
    x = middle.astype(jnp.float32)
    reduce_chip(1, pack_stats(jnp.sum(x, axis=0, keepdims=True), jnp.sum(x * x, axis=0, keepdims=True)))
    reduce_all(1)
    count = tm_n * rows_n * frames * height * width * (cout // GROUPS)
    a, b = affine(reduced(1), count, g2[...], s2[...])
    normalize(mx, sn, (1, 3, 1, 3), a, b)
    for n in range(5):
        normalize_halo(n, halo2[n], mx, sn, boxes[n], a, b)

    writes = []
    for rb in range(2):
        near = [sn[f : f + 2, r : r + height].reshape(size, cout) for f in (0, 1) for r in (rb, rb + 1)]
        lhs_s = jnp.concatenate(near, axis=1)
        far = [sn[0:3, r : r + height].reshape(3 * height * width, cout) for r in (rb, rb + 1)]
        lhs_r = jnp.concatenate(far, axis=1)
        s = [
            jnp.dot(lhs_s, w2[rb, k, 0:4].reshape(4 * cout, cout), preferred_element_type=jnp.float32)
            for k in range(TAPS)
        ]
        q = [
            jnp.dot(lhs_r, w2[rb, k, 4:6].reshape(2 * cout, cout), preferred_element_type=jnp.float32)
            for k in range(TAPS)
        ]
        for ta in range(2):
            skip = ta * height * width
            z = [s[k] + q[k][skip : skip + size] for k in range(TAPS)]
            pair = (after(z[0]) + z[1] + z[2], z[0] + z[1] + before(z[2]))
            for n in range(cout // LANES):
                part = slice(n * LANES, (n + 1) * LANES)
                for tc in range(2):
                    stage[n, pl.ds(tc, size, stride=2), :] = pair[tc][:, part]
                ob[rb, ta, :, :, :, part] = stage[n].astype(jnp.bfloat16).reshape(frames, height, 2 * width, LANES)
            for t in range(frames):
                for h in range(height):
                    write = pltpu.make_async_copy(
                        ob.at[rb, ta, t, h], out.at[2 * t + ta, 2 * h + rb], out_sem.at[rb, ta, t, h]
                    )
                    write.start()
                    writes.append(write)

    for c in writes:
        c.wait()
    for copies in (halo1, halo2):
        for n in range(5):
            pl.when(peers[n][0])(copies[n].wait_send)
    for which in range(2):
        for ref, n in ((red_core, 2 * which), (red_chip, 2 * which + 1)):
            rest = ref.at[which, 1 : ref.shape[1]]
            pltpu.make_async_copy(rest, rest, rs_sem.at[n]).wait()


def solution(mesh):
    tm_n, rows_n = mesh.shape["tm"], mesh.shape["rows"]

    def per_device(latent, gain1, shift1, kernel1, gain2, shift2, kernel2):
        frames, height, width, cin = latent.shape
        cout = kernel1.shape[-1]
        bf16, f32 = jnp.bfloat16, jnp.float32
        dma = pltpu.SemaphoreType.DMA
        return pl.pallas_call(
            functools.partial(kernel, tm_n, rows_n),
            out_shape=jax.ShapeDtypeStruct((2 * frames, 2 * height, 2 * width, cout), bf16),
            in_specs=[pl.BlockSpec(memory_space=pltpu.HBM)] * 7,
            out_specs=pl.BlockSpec(memory_space=pltpu.HBM),
            scratch_shapes=[
                pltpu.VMEM((frames + 2, height + 2, width, cin), bf16),
                pltpu.VMEM((frames + 2, height + 2, width, cin), bf16),
                pltpu.VMEM((TAPS, TAPS, TAPS, cin, cout), bf16),
                pltpu.VMEM((2, TAPS, 6, cout, cout), bf16),
                pltpu.VMEM((TAPS, TAPS, cout, cout), bf16),
                pltpu.VMEM((frames + 1, height + 2, width, cout), bf16),
                pltpu.VMEM((frames + 1, height + 2, width, cout), bf16),
                pltpu.VMEM((cout // LANES, 2 * frames * height * width, LANES), f32),
                pltpu.VMEM((2, 2, frames, height, 2 * width, cout), bf16),
                pltpu.VMEM((1, cin), f32),
                pltpu.VMEM((1, cin), f32),
                pltpu.VMEM((1, cout), f32),
                pltpu.VMEM((1, cout), f32),
                pltpu.VMEM((2, CORES, 1, LANES), f32),
                pltpu.VMEM((2, tm_n * rows_n // CORES, 1, LANES), f32),
                dma((5,)),
                dma((TAPS * TAPS,)),
                dma((TAPS * TAPS,)),
                dma((2, 2, frames, height)),
                dma((2, 5)),
                dma((2, 5)),
                dma((4,)),
                dma((4,)),
            ],
            compiler_params=pltpu.CompilerParams(
                collective_id=0, has_side_effects=True, vmem_limit_bytes=63 * 1024 * 1024
            ),
        )(
            latent, gain1.reshape(1, -1), shift1.reshape(1, -1), kernel1,
            gain2.reshape(1, -1), shift2.reshape(1, -1), kernel2,
        )

    placed = (P("tm", "rows", None, None), P(), P(), P(), P(), P(), P())
    return jax.shard_map(
        per_device, mesh=mesh, in_specs=placed, out_specs=P("tm", "rows", None, None), check_vma=False
    )
```

time: 204 us -> 34.2 us (0.17)
  the two profiles are of different devices: /device:TPU:38 before, /device:TPU:1 now
where the time goes in v1:
time: 34.2 us; the launch traced here: 34.1 us
  Pallas kernels  32 us (94%)
  local copies, waits for them, and re-layouts  2.06 us (6%)
    pallas_call x1, Pallas kernels, per_device(): pl.pallas_call(functools.partial(kernel, tm_n, rows_n), out_shape=jax.Sha...  32 us
    unnamed x1, local copies, waits for them, and re-layouts  2.06 us

profile of v1, /device:TPU:1, one launch (start us, length us, event | category | flops | bytes accessed | tf_op | source)
XLA Modules:
  0.0 34.1 jit_solution(13698776408066947669)
XLA Ops:
  0.0 32.0 %shard_map.73 = bf16[4,4,96,256]{3,2,1,0:T(8,128)(2,1)} custom-call(bf16[2,2,48,512]{3,2,1,0:T(8,128)(2,1)} %latent.1, f32[1,512]{1,0:T(1,128)} %bitcast.4, f32[1,512]{1,0:T(1,128)} %bitcast.5, bf16[3,3,3,512,256]{4,3,2,1,0:T(8,128)(2,1)} %kernel1.1, f32[1,256]{1,0:T(1,128)} %bitcast.6, f32[1,256]{1,0:T(1,128)} %bitcast.7, bf16[3,3,3,256,256]{4,3,2,1,0:T(8,128)(2,1)} %kernel2.1), custom_call_target="tpu_custom_call" | custom-call | tf_op jit(solution)/shard_map/pallas_call | solution.py:303
  32.0 2.1 %copy.9 = bf16[4,4,96,256]{3,2,1,0:T(8,128)(2,1)} copy(bf16[4,4,96,256]{3,2,1,0:T(8,128)(2,1)} %shard_map.73) | data formatting | bytes 1572864

commit v2 on v1

--- a/solution.py
+++ b/solution.py
@@ -81,8 +81,8 @@
 def kernel(
     tm_n, rows_n,
     latent, gain1, shift1, kernel1, gain2, shift2, kernel2, out,
-    lx, xn, w1, w2, w2m, mx, sn, stage, ob, g1, s1, g2, s2, red_core, red_chip,
-    load_sem, w1_sem, w2_sem, out_sem, hs_sem, hr_sem, rs_sem, rr_sem,
+    lx, xn, w1, w2, w2m, mx, sn, stage, g1, s1, g2, s2, red_core, red_chip,
+    load_sem, w1_sem, w2_sem, hs_sem, hr_sem, rs_sem, rr_sem,
 ):
     tm, row = lax.axis_index("tm"), lax.axis_index("rows")
     frames, height, width, cin = latent.shape
@@ -119,6 +119,9 @@
     partners = chips + [(tm_at(d), row_at(e)) for e in (-1, 1, 0) for d in (-1, 1)]
     for p in partners:
         pl.semaphore_signal(barrier, inc=1, device_id=p, device_id_type=MESH)
+    load.wait()
+    x = lx[2:4, 1:3].astype(jnp.float32).reshape(frames * height * width, cin)
+    red_core[0, 0] = pack_stats(jnp.sum(x, axis=0, keepdims=True), jnp.sum(x * x, axis=0, keepdims=True))
     pl.semaphore_wait(barrier, len(partners))
 
     both = jnp.logical_and
@@ -129,20 +132,27 @@
         (both(next_ok, up_ok), (tm_at(1), row_at(-1))),
         (both(next_ok, down_ok), (tm_at(1), row_at(1))),
     ]
+    first_core = lax.rem(tm, CORES) == 0
     arrives = [prev_ok, down_ok, up_ok, both(prev_ok, down_ok), both(prev_ok, up_ok)]
 
     def exchange(which, sources, targets):
         copies = []
         for n in range(5):
-            ok, device = peers[n]
+            device = peers[n][1]
             copy = pltpu.make_async_remote_copy(
                 src_ref=sources[n], dst_ref=targets[n],
                 send_sem=hs_sem.at[which, n], recv_sem=hr_sem.at[which, n],
                 device_id=device, device_id_type=MESH,
             )
-            pl.when(ok)(copy.start)
             copies.append(copy)
         return copies
+
+    def goes(copies, n):
+        return both(peers[n][0], jnp.logical_not(first_core)) if copies is halo1 and n >= 3 else peers[n][0]
+
+    def start(copies, which):
+        for n in which:
+            pl.when(goes(copies, n))(copies[n].start)
 
     def send(which, ref, n, device):
         pltpu.make_async_remote_copy(
@@ -156,10 +166,8 @@
         pltpu.make_async_copy(ref.at[1:n], ref.at[1:n], rr_sem.at[which]).wait()
         return jnp.sum(ref[...], axis=0)
 
-    def reduce_chip(which, value):
-        ref = red_core.at[which]
-        ref[0] = value
-        send(2 * which, ref, 1, twin)
+    def reduce_chip(which):
+        send(2 * which, red_core.at[which], 1, twin)
 
     def reduce_all(which):
         ref = red_chip.at[which]
@@ -176,10 +184,9 @@
         [latent, latent.at[:, 0:1], latent.at[:, 1:2], latent.at[:, 0:1], latent.at[:, 1:2]],
         [lx.at[a:b, c:d] for a, b, c, d in boxes],
     )
-    load.wait()
-    x = lx[2:4, 1:3].astype(jnp.float32).reshape(frames * height * width, cin)
-    reduce_chip(0, pack_stats(jnp.sum(x, axis=0, keepdims=True), jnp.sum(x * x, axis=0, keepdims=True)))
+    reduce_chip(0)
     reduce_all(0)
+    start(halo1, (1, 2, 3, 4, 0))
     for c in w2_loads:
         c.wait()
 
@@ -191,6 +198,17 @@
 
     for i in range(TAPS):
         merge(i)
+    forward = []
+    for n in (1, 2):
+        f0, f1, r0, r1 = boxes[n]
+        copy = pltpu.make_async_remote_copy(
+            src_ref=lx.at[f0:f1, r0:r1], dst_ref=lx.at[0:2, r0:r1],
+            send_sem=hs_sem.at[0, n + 2], recv_sem=hr_sem.at[0, n + 2],
+            device_id=twin, device_id_type=MESH,
+        )
+        pl.when(arrives[n])(halo1[n].wait_recv)
+        pl.when(both(arrives[n], first_core))(copy.start)
+        forward.append(copy)
     for c in small:
         c.wait()
     count = tm_n * rows_n * frames * height * width * (cin // GROUPS)
@@ -207,7 +225,8 @@
 
         @pl.when(arrives[n])
         def _():
-            copy.wait_recv()
+            if copy is not halo1[1] and copy is not halo1[2]:
+                copy.wait_recv()
             normalize(source, target, box, a, b)
 
         @pl.when(jnp.logical_not(arrives[n]))
@@ -241,8 +260,10 @@
         [mx.at[2:3, 1:3], mx.at[1:3, 1:2], mx.at[1:3, 2:3], mx.at[2:3, 1:2], mx.at[2:3, 2:3]],
         [mx.at[a:b, c:d] for a, b, c, d in boxes],
     )
+    start(halo2, range(5))
     x = middle.astype(jnp.float32)
-    reduce_chip(1, pack_stats(jnp.sum(x, axis=0, keepdims=True), jnp.sum(x * x, axis=0, keepdims=True)))
+    red_core[1, 0] = pack_stats(jnp.sum(x, axis=0, keepdims=True), jnp.sum(x * x, axis=0, keepdims=True))
+    reduce_chip(1)
     reduce_all(1)
     count = tm_n * rows_n * frames * height * width * (cout // GROUPS)
     a, b = affine(reduced(1), count, g2[...], s2[...])
@@ -250,7 +271,6 @@
     for n in range(5):
         normalize_halo(n, halo2[n], mx, sn, boxes[n], a, b)
 
-    writes = []
     for rb in range(2):
         near = [sn[f : f + 2, r : r + height].reshape(size, cout) for f in (0, 1) for r in (rb, rb + 1)]
         lhs_s = jnp.concatenate(near, axis=1)
@@ -272,20 +292,16 @@
                 part = slice(n * LANES, (n + 1) * LANES)
                 for tc in range(2):
                     stage[n, pl.ds(tc, size, stride=2), :] = pair[tc][:, part]
-                ob[rb, ta, :, :, :, part] = stage[n].astype(jnp.bfloat16).reshape(frames, height, 2 * width, LANES)
-            for t in range(frames):
-                for h in range(height):
-                    write = pltpu.make_async_copy(
-                        ob.at[rb, ta, t, h], out.at[2 * t + ta, 2 * h + rb], out_sem.at[rb, ta, t, h]
-                    )
-                    write.start()
-                    writes.append(write)
-
-    for c in writes:
-        c.wait()
+                full = stage[n].astype(jnp.bfloat16).reshape(frames, height, 2 * width, LANES)
+                for t in range(frames):
+                    for h in range(height):
+                        out[2 * t + ta, 2 * h + rb, :, part] = full[t, h]
+
     for copies in (halo1, halo2):
         for n in range(5):
-            pl.when(peers[n][0])(copies[n].wait_send)
+            pl.when(goes(copies, n))(copies[n].wait_send)
+    for n in (1, 2):
+        pl.when(both(arrives[n], first_core))(forward[n - 1].wait_send)
     for which in range(2):
         for ref, n in ((red_core, 2 * which), (red_chip, 2 * which + 1)):
             rest = ref.at[which, 1 : ref.shape[1]]
@@ -302,9 +318,9 @@
         dma = pltpu.SemaphoreType.DMA
         return pl.pallas_call(
             functools.partial(kernel, tm_n, rows_n),
-            out_shape=jax.ShapeDtypeStruct((2 * frames, 2 * height, 2 * width, cout), bf16),
+            out_shape=pltpu.VMEM((2 * frames, 2 * height, 2 * width, cout), bf16),
             in_specs=[pl.BlockSpec(memory_space=pltpu.HBM)] * 7,
-            out_specs=pl.BlockSpec(memory_space=pltpu.HBM),
+            out_specs=pl.BlockSpec(memory_space=pltpu.VMEM),
             scratch_shapes=[
                 pltpu.VMEM((frames + 2, height + 2, width, cin), bf16),
                 pltpu.VMEM((frames + 2, height + 2, width, cin), bf16),
@@ -314,7 +330,6 @@
                 pltpu.VMEM((frames + 1, height + 2, width, cout), bf16),
                 pltpu.VMEM((frames + 1, height + 2, width, cout), bf16),
                 pltpu.VMEM((cout // LANES, 2 * frames * height * width, LANES), f32),
-                pltpu.VMEM((2, 2, frames, height, 2 * width, cout), bf16),
                 pltpu.VMEM((1, cin), f32),
                 pltpu.VMEM((1, cin), f32),
                 pltpu.VMEM((1, cout), f32),
@@ -324,19 +339,21 @@
                 dma((5,)),
                 dma((TAPS * TAPS,)),
                 dma((TAPS * TAPS,)),
-                dma((2, 2, frames, height)),
                 dma((2, 5)),
                 dma((2, 5)),
                 dma((4,)),
                 dma((4,)),
             ],
             compiler_params=pltpu.CompilerParams(
-                collective_id=0, has_side_effects=True, vmem_limit_bytes=63 * 1024 * 1024
+                collective_id=0, has_side_effects=True, vmem_limit_bytes=48 * 1024 * 1024
             ),
-        )(
-            latent, gain1.reshape(1, -1), shift1.reshape(1, -1), kernel1,
-            gain2.reshape(1, -1), shift2.reshape(1, -1), kernel2,
-        )
+        )(*(
+            pltpu.with_memory_space_constraint(x, pltpu.HBM)
+            for x in (
+                latent, gain1.reshape(1, -1), shift1.reshape(1, -1), kernel1,
+                gain2.reshape(1, -1), shift2.reshape(1, -1), kernel2,
+            )
+        ))
 
     placed = (P("tm", "rows", None, None), P(), P(), P(), P(), P(), P())
     return jax.shard_map(

time: 34.2 us -> 30 us (0.88)
  Pallas kernels: 32 us -> 29 us
  local copies, waits for them, and re-layouts: 2.06 us -> 0.88 us
    pallas_call x1, Pallas kernels: 32 us -> 29 us  [per_device(): pl.pallas_call(functools.partial(kernel, tm_n, rows_n), out_shape=pltpu.V...]
    unnamed x1, local copies, waits for them, and re-layouts: 2.06 us -> 0.88 us
where the time goes in v2:
time: 30 us; the launch traced here: 29.9 us
  Pallas kernels  29 us (97%)
  local copies, waits for them, and re-layouts  0.88 us (3%)
    pallas_call x1, Pallas kernels, per_device(): pl.pallas_call(functools.partial(kernel, tm_n, rows_n), out_shape=pltpu.V...  29 us
    unnamed x1, local copies, waits for them, and re-layouts  0.88 us

profile of v2, /device:TPU:1, one launch (start us, length us, event | category | flops | bytes accessed | tf_op | source)
XLA Modules:
  0.0 29.9 jit_solution(12040630014756990475)
XLA Ops:
  0.0 29.0 %shard_map.73 = bf16[4,4,96,256]{3,2,1,0:T(8,128)(2,1)S(1)} custom-call(bf16[2,2,48,512]{3,2,1,0:T(8,128)(2,1)} %latent.1, f32[1,512]{1,0:T(1,128)} %bitcast.4, f32[1,512]{1,0:T(1,128)} %bitcast.5, bf16[3,3,3,512,256]{4,3,2,1,0:T(8,128)(2,1)} %kernel1.1, f32[1,256]{1,0:T(1,128)} %bitcast.6, f32[1,256]{1,0:T(1,128)} %bitcast.7, ...), custom_call_target="tpu_custom_call" | custom-call | tf_op jit(solution)/shard_map/pallas_call | solution.py:319
  29.0 0.9 %copy.9 = bf16[4,4,96,256]{3,2,1,0:T(8,128)(2,1)} copy(bf16[4,4,96,256]{3,2,1,0:T(8,128)(2,1)S(1)} %shard_map.73) | data formatting | bytes 1572864

commit v3 on v2

--- a/solution.py
+++ b/solution.py
@@ -16,61 +16,60 @@
 SIDE = 4
 
 
-def chip_partners(tm, row, tm_n, rows_n):
-    at_z = [lax.rem(tm + CORES * d, tm_n) for d in range(tm_n // CORES)]
-    at_y = [lax.rem(row - lax.rem(row, SIDE) + SIDE * d, rows_n) for d in range(rows_n // SIDE)]
-    at_x = [lax.rem(row + d, SIDE) for d in range(SIDE)]
+def partners_of(tm, row, tm_n, rows_n):
+    z_n, y_n = tm_n // CORES, rows_n // SIDE
+    core, x = lax.rem(tm, CORES), lax.rem(row, SIDE)
+    y = lax.div(row, SIDE)
+    at_z = [lax.rem(tm + CORES * d, tm_n) for d in range(z_n)]
+    at_x = [lax.rem(x + d, SIDE) for d in range(SIDE)]
+    pair = [y * SIDE, (y + 1 - 2 * lax.rem(y, 2)) * SIDE]
+    mirror = [y * SIDE, (y_n - 1 - y) * SIDE]
+    cores = [tm, tm + 1 - 2 * core]
     hops = lambda d, n: min(d, n - d)
-    steps = [
-        (-hops(dz, len(at_z)) - hops(dy, len(at_y)) - hops(dx, SIDE), dz, dy, dx)
-        for dz in range(len(at_z))
-        for dy in range(len(at_y))
-        for dx in range(SIDE)
-        if dz or dy or dx
-    ]
-    return [(at_z[dz], at_y[dy] + at_x[dx]) for _, dz, dy, dx in sorted(steps)]
-
-
-def lane_sums(x, size):
-    lane = lax.broadcasted_iota(jnp.int32, x.shape, 1)
-    d = 1
-    while d < size:
-        other = jnp.where((lane & d) == 0, pltpu.roll(x, LANES - d, 1), pltpu.roll(x, d, 1))
-        x = x + other
-        d *= 2
-    return x
-
-
-def diagonal(size):
-    lane = lax.broadcasted_iota(jnp.int32, (8, LANES), 1)
-    sub = lax.broadcasted_iota(jnp.int32, (8, LANES), 0)
-    return (lane & (size - 1)) == sub
-
-
-def pack_stats(total, square):
-    blocks = total.shape[1] // LANES
-    size = total.shape[1] // GROUPS
-    sub = lax.broadcasted_iota(jnp.int32, (8, LANES), 0)
-    rows = jnp.zeros((8, LANES), jnp.float32)
-    for v in range(blocks):
-        part = slice(v * LANES, (v + 1) * LANES)
-        rows = jnp.where(sub == v, total[:, part], rows)
-        rows = jnp.where(sub == blocks + v, square[:, part], rows)
-    rows = lane_sums(rows, size)
-    return jnp.sum(jnp.where(diagonal(size), rows, 0.0), axis=0, keepdims=True)
-
-
-def affine(packed, count, gain, shift):
+
+    def ordered(places):
+        return [device for _, _, device in sorted(places, key=lambda p: p[:2])[:-1]]
+
+    near = ordered([
+        (-hops(dx, SIDE) - dy, -n, (cores[n], pair[dy] + at_x[dx]))
+        for dx in range(SIDE) for dy in range(2) for n in range(CORES)
+    ])
+    across = ordered([
+        (-hops(dz, z_n) - dy, -dz, (at_z[dz], mirror[dy] + x)) for dz in range(z_n) for dy in range(2)
+    ])
+    return near, across
+
+
+def thirds(x):
+    high = x.astype(jnp.bfloat16).astype(jnp.float32)
+    rest = x - high
+    middle = rest.astype(jnp.bfloat16).astype(jnp.float32)
+    return jnp.concatenate([high, middle, rest - middle, jnp.zeros_like(x)], axis=0).astype(jnp.bfloat16)
+
+
+def member(shape, size, axis):
+    chan = lax.broadcasted_iota(jnp.int32, shape, axis)
+    group = lax.broadcasted_iota(jnp.int32, shape, 1 - axis)
+    return (lax.div(chan, size) == group).astype(jnp.float32).astype(jnp.bfloat16)
+
+
+def pack_stats(x, groups):
+    parts = x.reshape(x.shape[0] // 8, 8, x.shape[1])
+    sums = jnp.concatenate([jnp.sum(parts, axis=0), jnp.sum(parts * parts, axis=0)], axis=1)
+    return jnp.sum(jnp.dot(thirds(sums), groups, preferred_element_type=jnp.float32), axis=0, keepdims=True)
+
+
+def affine(packed, count, gain, shift, channels):
     chans = gain.shape[1]
-    blocks, size = chans // LANES, chans // GROUPS
-    rows = jnp.where(diagonal(size), jnp.broadcast_to(packed, (8, LANES)), 0.0)
-    rows = lane_sums(rows, size) * (1.0 / count)
-    mean = rows
-    spread = pltpu.roll(rows, 8 - blocks, 0) - mean * mean
-    scale = lax.rsqrt(spread + EPS) * 0.5
-    a = jnp.concatenate([scale[v : v + 1] for v in range(blocks)], axis=1) * gain
-    m = jnp.concatenate([mean[v : v + 1] for v in range(blocks)], axis=1)
-    return a, shift * 0.5 - m * a
+    first = lax.broadcasted_iota(jnp.int32, (8, LANES), 0) == 0
+    spread_out = jnp.dot(
+        thirds(jnp.where(first, packed * (1.0 / count), 0.0)), channels, preferred_element_type=jnp.float32
+    )
+    moments = jnp.sum(spread_out, axis=0, keepdims=True)
+    mean = moments[:, :chans]
+    spread = moments[:, chans:] - mean * mean
+    a = lax.rsqrt(spread + EPS) * 0.5 * gain
+    return a, shift * 0.5 - mean * a
 
 
 def activate(x, a, b):
@@ -81,12 +80,13 @@
 def kernel(
     tm_n, rows_n,
     latent, gain1, shift1, kernel1, gain2, shift2, kernel2, out,
-    lx, xn, w1, w2, w2m, mx, sn, stage, g1, s1, g2, s2, red_core, red_chip,
+    lx, xn, w1, w2, w2m, mx, sn, stage, g1, s1, g2, s2, groups1, channels1, groups2, channels2, red_near, red_across, red_all,
     load_sem, w1_sem, w2_sem, hs_sem, hr_sem, rs_sem, rr_sem,
 ):
     tm, row = lax.axis_index("tm"), lax.axis_index("rows")
     frames, height, width, cin = latent.shape
     cout = kernel1.shape[-1]
+    place = row * tm_n + tm
     up_ok, down_ok = row > 0, row < rows_n - 1
     prev_ok, next_ok = tm > 0, tm < tm_n - 1
     tm_at = lambda d: lax.rem(tm + d + tm_n, tm_n)
@@ -95,6 +95,14 @@
     own = lx.at[2:4, 1:3]
     load = pltpu.make_async_copy(latent, own, load_sem.at[0])
     load.start()
+
+    barrier = pltpu.get_barrier_semaphore()
+    near, across = partners_of(tm, row, tm_n, rows_n)
+    twin = (tm + 1 - 2 * lax.rem(tm, CORES), row)
+    partners = [(tm_at(d), row_at(e)) for e in (-1, 1, 0) for d in (-1, 1)]
+    partners = near + across + partners + [(tm, row_at(e)) for e in (-1, 1)]
+    for p in partners:
+        pl.semaphore_signal(barrier, inc=1, device_id=p, device_id_type=MESH)
     small = [
         pltpu.make_async_copy(src, dst, load_sem.at[1 + n])
         for n, (src, dst) in enumerate(((gain1, g1), (shift1, s1), (gain2, g2), (shift2, s2)))
@@ -112,16 +120,10 @@
             w1_loads.append(pltpu.make_async_copy(kernel1.at[i, :, k], w1.at[k, i], w1_sem.at[TAPS * i + k]))
     for c in w2_loads + w1_loads:
         c.start()
-
-    barrier = pltpu.get_barrier_semaphore()
-    chips = chip_partners(tm, row, tm_n, rows_n)
-    twin = (tm + 1 - 2 * lax.rem(tm, CORES), row)
-    partners = chips + [(tm_at(d), row_at(e)) for e in (-1, 1, 0) for d in (-1, 1)]
-    for p in partners:
-        pl.semaphore_signal(barrier, inc=1, device_id=p, device_id_type=MESH)
     load.wait()
     x = lx[2:4, 1:3].astype(jnp.float32).reshape(frames * height * width, cin)
-    red_core[0, 0] = pack_stats(jnp.sum(x, axis=0, keepdims=True), jnp.sum(x * x, axis=0, keepdims=True))
+    groups1[...] = member(groups1.shape, cin // GROUPS, 0)
+    red_near[0] = pack_stats(x, groups1[...])
     pl.semaphore_wait(barrier, len(partners))
 
     both = jnp.logical_and
@@ -166,17 +168,9 @@
         pltpu.make_async_copy(ref.at[1:n], ref.at[1:n], rr_sem.at[which]).wait()
         return jnp.sum(ref[...], axis=0)
 
-    def reduce_chip(which):
-        send(2 * which, red_core.at[which], 1, twin)
-
-    def reduce_all(which):
-        ref = red_chip.at[which]
-        ref[0] = arrived(2 * which, red_core.at[which])
-        for n, device in enumerate(chips):
-            send(2 * which + 1, ref, n + 1, device)
-
-    def reduced(which):
-        return arrived(2 * which + 1, red_chip.at[which])
+    def send_all(which, ref, devices):
+        for n, device in enumerate(devices):
+            send(which, ref, n + 1, device)
 
     boxes = [(0, 2, 1, 3), (2, 4, 3, 4), (2, 4, 0, 1), (0, 2, 3, 4), (0, 2, 0, 1)]
     halo1 = exchange(
@@ -184,9 +178,13 @@
         [latent, latent.at[:, 0:1], latent.at[:, 1:2], latent.at[:, 0:1], latent.at[:, 1:2]],
         [lx.at[a:b, c:d] for a, b, c, d in boxes],
     )
-    reduce_chip(0)
-    reduce_all(0)
+    send_all(0, red_near, near)
     start(halo1, (1, 2, 3, 4, 0))
+    channels1[...] = member(channels1.shape, cin // GROUPS, 1)
+    groups2[...] = member(groups2.shape, cout // GROUPS, 0)
+    channels2[...] = member(channels2.shape, cout // GROUPS, 1)
+    red_across[0] = arrived(0, red_near)
+    send_all(1, red_across, across)
     for c in w2_loads:
         c.wait()
 
@@ -212,7 +210,7 @@
     for c in small:
         c.wait()
     count = tm_n * rows_n * frames * height * width * (cin // GROUPS)
-    a, b = affine(reduced(0), count, g1[...], s1[...])
+    a, b = affine(arrived(1, red_across), count, g1[...], s1[...], channels1[...])
 
     def normalize(source, target, box, a, b):
         f0, f1, r0, r1 = box
@@ -260,13 +258,20 @@
         [mx.at[2:3, 1:3], mx.at[1:3, 1:2], mx.at[1:3, 2:3], mx.at[2:3, 1:2], mx.at[2:3, 2:3]],
         [mx.at[a:b, c:d] for a, b, c, d in boxes],
     )
+    x = middle.astype(jnp.float32)
+    red_all[place] = pack_stats(x, groups2[...])
+    @pl.loop(0, tm_n * rows_n - 1)
+    def _(n):
+        to = n + (place <= n).astype(jnp.int32)
+        pltpu.make_async_remote_copy(
+            src_ref=red_all.at[place], dst_ref=red_all.at[place],
+            send_sem=rs_sem.at[2], recv_sem=rr_sem.at[2],
+            device_id=(lax.rem(to, tm_n), lax.div(to, tm_n)), device_id_type=MESH,
+        ).start()
+
     start(halo2, range(5))
-    x = middle.astype(jnp.float32)
-    red_core[1, 0] = pack_stats(jnp.sum(x, axis=0, keepdims=True), jnp.sum(x * x, axis=0, keepdims=True))
-    reduce_chip(1)
-    reduce_all(1)
     count = tm_n * rows_n * frames * height * width * (cout // GROUPS)
-    a, b = affine(reduced(1), count, g2[...], s2[...])
+    a, b = affine(arrived(2, red_all), count, g2[...], s2[...], channels2[...])
     normalize(mx, sn, (1, 3, 1, 3), a, b)
     for n in range(5):
         normalize_halo(n, halo2[n], mx, sn, boxes[n], a, b)
@@ -291,8 +296,8 @@
             for n in range(cout // LANES):
                 part = slice(n * LANES, (n + 1) * LANES)
                 for tc in range(2):
-                    stage[n, pl.ds(tc, size, stride=2), :] = pair[tc][:, part]
-                full = stage[n].astype(jnp.bfloat16).reshape(frames, height, 2 * width, LANES)
+                    stage[rb, ta, n, pl.ds(tc, size, stride=2), :] = pair[tc][:, part]
+                full = stage[rb, ta, n].astype(jnp.bfloat16).reshape(frames, height, 2 * width, LANES)
                 for t in range(frames):
                     for h in range(height):
                         out[2 * t + ta, 2 * h + rb, :, part] = full[t, h]
@@ -302,10 +307,9 @@
             pl.when(goes(copies, n))(copies[n].wait_send)
     for n in (1, 2):
         pl.when(both(arrives[n], first_core))(forward[n - 1].wait_send)
-    for which in range(2):
-        for ref, n in ((red_core, 2 * which), (red_chip, 2 * which + 1)):
-            rest = ref.at[which, 1 : ref.shape[1]]
-            pltpu.make_async_copy(rest, rest, rs_sem.at[n]).wait()
+    for which, ref in enumerate((red_near, red_across, red_all)):
+        rest = ref.at[1 : ref.shape[0]]
+        pltpu.make_async_copy(rest, rest, rs_sem.at[which]).wait()
 
 
 def solution(mesh):
@@ -329,20 +333,25 @@
                 pltpu.VMEM((TAPS, TAPS, cout, cout), bf16),
                 pltpu.VMEM((frames + 1, height + 2, width, cout), bf16),
                 pltpu.VMEM((frames + 1, height + 2, width, cout), bf16),
-                pltpu.VMEM((cout // LANES, 2 * frames * height * width, LANES), f32),
+                pltpu.VMEM((2, 2, cout // LANES, 2 * frames * height * width, LANES), f32),
                 pltpu.VMEM((1, cin), f32),
                 pltpu.VMEM((1, cin), f32),
                 pltpu.VMEM((1, cout), f32),
                 pltpu.VMEM((1, cout), f32),
-                pltpu.VMEM((2, CORES, 1, LANES), f32),
-                pltpu.VMEM((2, tm_n * rows_n // CORES, 1, LANES), f32),
+                pltpu.VMEM((2 * cin, LANES), bf16),
+                pltpu.VMEM((LANES, 2 * cin), bf16),
+                pltpu.VMEM((2 * cout, LANES), bf16),
+                pltpu.VMEM((LANES, 2 * cout), bf16),
+                pltpu.VMEM((2 * SIDE * CORES, 1, LANES), f32),
+                pltpu.VMEM((2 * tm_n // CORES, 1, LANES), f32),
+                pltpu.VMEM((tm_n * rows_n, 1, LANES), f32),
                 dma((5,)),
                 dma((TAPS * TAPS,)),
                 dma((TAPS * TAPS,)),
                 dma((2, 5)),
                 dma((2, 5)),
-                dma((4,)),
-                dma((4,)),
+                dma((3,)),
+                dma((3,)),
             ],
             compiler_params=pltpu.CompilerParams(
                 collective_id=0, has_side_effects=True, vmem_limit_bytes=48 * 1024 * 1024

time: 30 us -> 29.2 us (0.973)
  Pallas kernels: 29 us -> 28.2 us
    pallas_call x1, Pallas kernels: 29 us -> 28.2 us  [per_device(): pl.pallas_call(functools.partial(kernel, tm_n, rows_n), out_shape=pltpu.V...]
where the time goes in v3:
time: 29.2 us; the launch traced here: 29.1 us
  Pallas kernels  28.2 us (97%)
  local copies, waits for them, and re-layouts  0.88 us (3%)
    pallas_call x1, Pallas kernels, per_device(): pl.pallas_call(functools.partial(kernel, tm_n, rows_n), out_shape=pltpu.V...  28.2 us
    unnamed x1, local copies, waits for them, and re-layouts  0.88 us

profile of v3, /device:TPU:1, one launch (start us, length us, event | category | flops | bytes accessed | tf_op | source)
XLA Modules:
  0.0 29.1 jit_solution(51895338439208516)
XLA Ops:
  0.0 28.2 %shard_map.73 = bf16[4,4,96,256]{3,2,1,0:T(8,128)(2,1)S(1)} custom-call(bf16[2,2,48,512]{3,2,1,0:T(8,128)(2,1)} %latent.1, f32[1,512]{1,0:T(1,128)} %bitcast.4, f32[1,512]{1,0:T(1,128)} %bitcast.5, bf16[3,3,3,512,256]{4,3,2,1,0:T(8,128)(2,1)} %kernel1.1, f32[1,256]{1,0:T(1,128)} %bitcast.6, f32[1,256]{1,0:T(1,128)} %bitcast.7, ...), custom_call_target="tpu_custom_call" | custom-call | tf_op jit(solution)/shard_map/pallas_call | solution.py:323
  28.2 0.9 %copy.9 = bf16[4,4,96,256]{3,2,1,0:T(8,128)(2,1)} copy(bf16[4,4,96,256]{3,2,1,0:T(8,128)(2,1)S(1)} %shard_map.73) | data formatting | bytes 1572864

commit v4 on v3

--- a/solution.py
+++ b/solution.py
@@ -79,8 +79,8 @@
 
 def kernel(
     tm_n, rows_n,
-    latent, gain1, shift1, kernel1, gain2, shift2, kernel2, out,
-    lx, xn, w1, w2, w2m, mx, sn, stage, g1, s1, g2, s2, groups1, channels1, groups2, channels2, red_near, red_across, red_all,
+    latent, gain1, shift1, kernel1, gain2, shift2, kernel2, sn, w2,
+    lx, xn, w1, w2m, mx, g1, s1, g2, s2, groups1, channels1, groups2, channels2, red_near, red_across, red_all,
     load_sem, w1_sem, w2_sem, hs_sem, hr_sem, rs_sem, rr_sem,
 ):
     tm, row = lax.axis_index("tm"), lax.axis_index("rows")
@@ -276,6 +276,23 @@
     for n in range(5):
         normalize_halo(n, halo2[n], mx, sn, boxes[n], a, b)
 
+    for copies in (halo1, halo2):
+        for n in range(5):
+            pl.when(goes(copies, n))(copies[n].wait_send)
+    for n in (1, 2):
+        pl.when(both(arrives[n], first_core))(forward[n - 1].wait_send)
+    for which, ref in enumerate((red_near, red_across, red_all)):
+        rest = ref.at[1 : ref.shape[0]]
+        pltpu.make_async_copy(rest, rest, rs_sem.at[which]).wait()
+
+
+def second_conv(sn, w2, out, stage, ob, out_sem):
+    frames, height, width, cout = sn.shape[0] - 1, sn.shape[1] - 2, sn.shape[2], sn.shape[3]
+    size = frames * height * width
+    column = lax.rem(lax.broadcasted_iota(jnp.int32, (size, cout), 0), width)
+    after = lambda y: jnp.where(column == 0, 0.0, pltpu.roll(y, 1, 0))
+    before = lambda y: jnp.where(column == width - 1, 0.0, pltpu.roll(y, size - 1, 0))
+    writes = []
     for rb in range(2):
         near = [sn[f : f + 2, r : r + height].reshape(size, cout) for f in (0, 1) for r in (rb, rb + 1)]
         lhs_s = jnp.concatenate(near, axis=1)
@@ -298,18 +315,16 @@
                 for tc in range(2):
                     stage[rb, ta, n, pl.ds(tc, size, stride=2), :] = pair[tc][:, part]
                 full = stage[rb, ta, n].astype(jnp.bfloat16).reshape(frames, height, 2 * width, LANES)
-                for t in range(frames):
-                    for h in range(height):
-                        out[2 * t + ta, 2 * h + rb, :, part] = full[t, h]
-
-    for copies in (halo1, halo2):
-        for n in range(5):
-            pl.when(goes(copies, n))(copies[n].wait_send)
-    for n in (1, 2):
-        pl.when(both(arrives[n], first_core))(forward[n - 1].wait_send)
-    for which, ref in enumerate((red_near, red_across, red_all)):
-        rest = ref.at[1 : ref.shape[0]]
-        pltpu.make_async_copy(rest, rest, rs_sem.at[which]).wait()
+                ob[rb, ta, :, :, :, part] = full
+            for t in range(frames):
+                for h in range(height):
+                    write = pltpu.make_async_copy(
+                        ob.at[rb, ta, t, h], out.at[2 * t + ta, 2 * h + rb], out_sem.at[rb, ta, t, h]
+                    )
+                    write.start()
+                    writes.append(write)
+    for write in writes:
+        write.wait()
 
 
 def solution(mesh):
@@ -320,20 +335,20 @@
         cout = kernel1.shape[-1]
         bf16, f32 = jnp.bfloat16, jnp.float32
         dma = pltpu.SemaphoreType.DMA
-        return pl.pallas_call(
+        padded, merged = pl.pallas_call(
             functools.partial(kernel, tm_n, rows_n),
-            out_shape=pltpu.VMEM((2 * frames, 2 * height, 2 * width, cout), bf16),
+            out_shape=(
+                pltpu.VMEM((frames + 1, height + 2, width, cout), bf16),
+                pltpu.VMEM((2, TAPS, 6, cout, cout), bf16),
+            ),
             in_specs=[pl.BlockSpec(memory_space=pltpu.HBM)] * 7,
-            out_specs=pl.BlockSpec(memory_space=pltpu.VMEM),
+            out_specs=(pl.BlockSpec(memory_space=pltpu.VMEM),) * 2,
             scratch_shapes=[
                 pltpu.VMEM((frames + 2, height + 2, width, cin), bf16),
                 pltpu.VMEM((frames + 2, height + 2, width, cin), bf16),
                 pltpu.VMEM((TAPS, TAPS, TAPS, cin, cout), bf16),
-                pltpu.VMEM((2, TAPS, 6, cout, cout), bf16),
                 pltpu.VMEM((TAPS, TAPS, cout, cout), bf16),
                 pltpu.VMEM((frames + 1, height + 2, width, cout), bf16),
-                pltpu.VMEM((frames + 1, height + 2, width, cout), bf16),
-                pltpu.VMEM((2, 2, cout // LANES, 2 * frames * height * width, LANES), f32),
                 pltpu.VMEM((1, cin), f32),
                 pltpu.VMEM((1, cin), f32),
                 pltpu.VMEM((1, cout), f32),
@@ -363,6 +378,18 @@
                 gain2.reshape(1, -1), shift2.reshape(1, -1), kernel2,
             )
         ))
+        return pl.pallas_call(
+            second_conv,
+            out_shape=pltpu.HBM((2 * frames, 2 * height, 2 * width, cout), bf16),
+            in_specs=[pl.BlockSpec(memory_space=pltpu.VMEM)] * 2,
+            out_specs=pl.BlockSpec(memory_space=pltpu.HBM),
+            scratch_shapes=[
+                pltpu.VMEM((2, 2, cout // LANES, 2 * frames * height * width, LANES), f32),
+                pltpu.VMEM((2, 2, frames, height, 2 * width, cout), bf16),
+                dma((2, 2, frames, height)),
+            ],
+            compiler_params=pltpu.CompilerParams(vmem_limit_bytes=32 * 1024 * 1024),
+        )(padded, merged)
 
     placed = (P("tm", "rows", None, None), P(), P(), P(), P(), P(), P())
     return jax.shard_map(

time: 29.2 us -> 28.4 us (0.973)
  local copies, waits for them, and re-layouts: 0.88 us -> 0 us
    unnamed x1 -> x0, local copies, waits for them, and re-layouts: 0.88 us -> none
    pallas_call x1 -> x2, Pallas kernels: 28.2 us -> 28.3 us  [the longest x1 25.9 us: per_device(): pl.pallas_call(functools.partial(kernel, tm_n, rows_n), out_shape=(pltpu....]
where the time goes in v4:
time: 28.4 us; the launch traced here: 28.3 us
  Pallas kernels  28.3 us (100%)
    pallas_call x1, Pallas kernels, per_device(): pl.pallas_call(functools.partial(kernel, tm_n, rows_n), out_shape=(pltpu....  25.9 us
    pallas_call x1, Pallas kernels, per_device(): pl.pallas_call(second_conv, out_shape=pltpu.HBM((2 * frames, 2 * height,...  2.39 us

profile of v4, /device:TPU:1, one launch (start us, length us, event | category | flops | bytes accessed | tf_op | source)
XLA Modules:
  0.0 28.3 jit_solution(1169921383047694313)
XLA Ops:
  0.0 25.9 %shard_map.73 = (bf16[3,4,48,256]{3,2,1,0:T(8,128)(2,1)S(1)}, bf16[2,3,6,256,256]{4,3,2,1,0:T(8,128)(2,1)S(1)}) custom-call(bf16[2,2,48,512]{3,2,1,0:T(8,128)(2,1)} %latent.1, f32[1,512]{1,0:T(1,128)} %bitcast.4, f32[1,512]{1,0:T(1,128)} %bitcast.5, bf16[3,3,3,512,256]{4,3,2,1,0:T(8,128)(2,1)} %kernel1.1, f32[1,256]{1,0:T(1,128)} %bitcast.6, ...), custom_call_target="tpu_custom_call" | custom-call | tf_op jit(solution)/shard_map/pallas_call | solution.py:338
  25.9 2.4 %shard_map.74 = bf16[4,4,96,256]{3,2,1,0:T(8,128)(2,1)} custom-call(bf16[3,4,48,256]{3,2,1,0:T(8,128)(2,1)S(1)} %get-tuple-element.7.sn, bf16[2,3,6,256,256]{4,3,2,1,0:T(8,128)(2,1)S(1)} %get-tuple-element.8.w2), custom_call_target="tpu_custom_call" | custom-call | tf_op jit(solution)/shard_map/pallas_call | solution.py:381

commit v5 on v4

--- a/solution.py
+++ b/solution.py
@@ -100,7 +100,7 @@
     near, across = partners_of(tm, row, tm_n, rows_n)
     twin = (tm + 1 - 2 * lax.rem(tm, CORES), row)
     partners = [(tm_at(d), row_at(e)) for e in (-1, 1, 0) for d in (-1, 1)]
-    partners = near + across + partners + [(tm, row_at(e)) for e in (-1, 1)]
+    partners = (near + across + partners + [(tm, row_at(e)) for e in (-1, 1)])[::-1]
     for p in partners:
         pl.semaphore_signal(barrier, inc=1, device_id=p, device_id_type=MESH)
     small = [
@@ -166,7 +166,11 @@
     def arrived(which, ref):
         n = ref.shape[0]
         pltpu.make_async_copy(ref.at[1:n], ref.at[1:n], rr_sem.at[which]).wait()
-        return jnp.sum(ref[...], axis=0)
+        parts = ref[...]
+        while n > 1:
+            n //= 2
+            parts = parts[:n] + parts[n:]
+        return parts[0]
 
     def send_all(which, ref, devices):
         for n, device in enumerate(devices):
@@ -310,14 +314,16 @@
             skip = ta * height * width
             z = [s[k] + q[k][skip : skip + size] for k in range(TAPS)]
             pair = (after(z[0]) + z[1] + z[2], z[0] + z[1] + before(z[2]))
-            for n in range(cout // LANES):
-                part = slice(n * LANES, (n + 1) * LANES)
-                for tc in range(2):
-                    stage[rb, ta, n, pl.ds(tc, size, stride=2), :] = pair[tc][:, part]
-                full = stage[rb, ta, n].astype(jnp.bfloat16).reshape(frames, height, 2 * width, LANES)
-                ob[rb, ta, :, :, :, part] = full
             for t in range(frames):
                 for h in range(height):
+                    place = (t * height + h) * width
+                    for n in range(cout // LANES):
+                        part = slice(n * LANES, (n + 1) * LANES)
+                        for tc in range(2):
+                            rows = pl.ds(2 * place + tc, width, stride=2)
+                            stage[rb, ta, n, rows, :] = pair[tc][place : place + width, part]
+                        full = stage[rb, ta, n, 2 * place : 2 * (place + width)]
+                        ob[rb, ta, t, h, :, part] = full.astype(jnp.bfloat16)
                     write = pltpu.make_async_copy(
                         ob.at[rb, ta, t, h], out.at[2 * t + ta, 2 * h + rb], out_sem.at[rb, ta, t, h]
                     )

time: 28.4 us -> 28.1 us (0.989)
  Pallas kernels: 28.3 us -> 28 us
where the time goes in v5:
time: 28.1 us; the launch traced here: 28 us
  Pallas kernels  28 us (100%)
    pallas_call x1, Pallas kernels, per_device(): pl.pallas_call(functools.partial(kernel, tm_n, rows_n), out_shape=(pltpu....  25.6 us
    pallas_call x1, Pallas kernels, per_device(): pl.pallas_call(second_conv, out_shape=pltpu.HBM((2 * frames, 2 * height,...  2.35 us

profile of v5, /device:TPU:1, one launch (start us, length us, event | category | flops | bytes accessed | tf_op | source)
XLA Modules:
  0.0 28.0 jit_solution(857885286617461788)
XLA Ops:
  0.0 25.6 %shard_map.73 = (bf16[3,4,48,256]{3,2,1,0:T(8,128)(2,1)S(1)}, bf16[2,3,6,256,256]{4,3,2,1,0:T(8,128)(2,1)S(1)}) custom-call(bf16[2,2,48,512]{3,2,1,0:T(8,128)(2,1)} %latent.1, f32[1,512]{1,0:T(1,128)} %bitcast.4, f32[1,512]{1,0:T(1,128)} %bitcast.5, bf16[3,3,3,512,256]{4,3,2,1,0:T(8,128)(2,1)} %kernel1.1, f32[1,256]{1,0:T(1,128)} %bitcast.6, ...), custom_call_target="tpu_custom_call" | custom-call | tf_op jit(solution)/shard_map/pallas_call | solution.py:344
  25.6 2.4 %shard_map.74 = bf16[4,4,96,256]{3,2,1,0:T(8,128)(2,1)} custom-call(bf16[3,4,48,256]{3,2,1,0:T(8,128)(2,1)S(1)} %get-tuple-element.7.sn, bf16[2,3,6,256,256]{4,3,2,1,0:T(8,128)(2,1)S(1)} %get-tuple-element.8.w2), custom_call_target="tpu_custom_call" | custom-call | tf_op jit(solution)/shard_map/pallas_call | solution.py:387

commit v6 on v5

--- a/solution.py
+++ b/solution.py
@@ -249,11 +249,11 @@
     lhs = jnp.concatenate(
         [xn[i : i + frames, j : j + height].reshape(size, cin) for i in range(TAPS) for j in range(TAPS)], axis=1
     )
-    y = [
-        jnp.dot(lhs, w1[k].reshape(TAPS * TAPS * cin, cout), preferred_element_type=jnp.float32)
-        for k in range(TAPS)
-    ]
-    middle = (after(y[0]) + y[1] + before(y[2])).astype(jnp.bfloat16)
+    y = {
+        k: jnp.dot(lhs, w1[k].reshape(TAPS * TAPS * cin, cout), preferred_element_type=jnp.float32)
+        for k in (0, 2, 1)
+    }
+    middle = (after(y[0]) + before(y[2]) + y[1]).astype(jnp.bfloat16)
     mx[1:3, 1:3] = middle.reshape(frames, height, width, cout)
 
     boxes = [(0, 1, 1, 3), (1, 3, 3, 4), (1, 3, 0, 1), (0, 1, 3, 4), (0, 1, 0, 1)]
@@ -302,18 +302,14 @@
         lhs_s = jnp.concatenate(near, axis=1)
         far = [sn[0:3, r : r + height].reshape(3 * height * width, cout) for r in (rb, rb + 1)]
         lhs_r = jnp.concatenate(far, axis=1)
-        s = [
-            jnp.dot(lhs_s, w2[rb, k, 0:4].reshape(4 * cout, cout), preferred_element_type=jnp.float32)
-            for k in range(TAPS)
-        ]
-        q = [
-            jnp.dot(lhs_r, w2[rb, k, 4:6].reshape(2 * cout, cout), preferred_element_type=jnp.float32)
-            for k in range(TAPS)
-        ]
+        s, q = {}, {}
+        for k in (0, 2, 1):
+            s[k] = jnp.dot(lhs_s, w2[rb, k, 0:4].reshape(4 * cout, cout), preferred_element_type=jnp.float32)
+            q[k] = jnp.dot(lhs_r, w2[rb, k, 4:6].reshape(2 * cout, cout), preferred_element_type=jnp.float32)
         for ta in range(2):
             skip = ta * height * width
             z = [s[k] + q[k][skip : skip + size] for k in range(TAPS)]
-            pair = (after(z[0]) + z[1] + z[2], z[0] + z[1] + before(z[2]))
+            pair = (after(z[0]) + z[2] + z[1], z[0] + before(z[2]) + z[1])
             for t in range(frames):
                 for h in range(height):
                     place = (t * height + h) * width

time: 28.1 us -> 28.1 us (level)
  no operation moved by 1% of the time
where the time goes in v6:
time: 28.1 us; the launch traced here: 28 us
  Pallas kernels  28 us (100%)
    pallas_call x1, Pallas kernels, per_device(): pl.pallas_call(functools.partial(kernel, tm_n, rows_n), out_shape=(pltpu....  25.6 us
    pallas_call x1, Pallas kernels, per_device(): pl.pallas_call(second_conv, out_shape=pltpu.HBM((2 * frames, 2 * height,...  2.34 us

profile of v6, /device:TPU:1, one launch (start us, length us, event | category | flops | bytes accessed | tf_op | source)
XLA Modules:
  0.0 28.0 jit_solution(2910139755632128826)
XLA Ops:
  0.0 25.6 %shard_map.73 = (bf16[3,4,48,256]{3,2,1,0:T(8,128)(2,1)S(1)}, bf16[2,3,6,256,256]{4,3,2,1,0:T(8,128)(2,1)S(1)}) custom-call(bf16[2,2,48,512]{3,2,1,0:T(8,128)(2,1)} %latent.1, f32[1,512]{1,0:T(1,128)} %bitcast.4, f32[1,512]{1,0:T(1,128)} %bitcast.5, bf16[3,3,3,512,256]{4,3,2,1,0:T(8,128)(2,1)} %kernel1.1, f32[1,256]{1,0:T(1,128)} %bitcast.6, ...), custom_call_target="tpu_custom_call" | custom-call | tf_op jit(solution)/shard_map/pallas_call | solution.py:340
  25.6 2.3 %shard_map.74 = bf16[4,4,96,256]{3,2,1,0:T(8,128)(2,1)} custom-call(bf16[3,4,48,256]{3,2,1,0:T(8,128)(2,1)S(1)} %get-tuple-element.7.sn, bf16[2,3,6,256,256]{4,3,2,1,0:T(8,128)(2,1)S(1)} %get-tuple-element.8.w2), custom_call_target="tpu_custom_call" | custom-call | tf_op jit(solution)/shard_map/pallas_call | solution.py:383
